TPU v7x, 256 devices: a whole 4x4x8 slice. The times are simulated.
256 devices in a mesh: lat: 32 (over x_hi, z, core), chan: 8 (over y, x_lo).
Axes of the slice: x: 4 (x_hi: 2, x_lo: 2; x = x_hi * 2 + x_lo), y: 4, z: 8, core: 2. Of those that a mesh axis runs over, the one named last changes fastest.
Arguments:
- fields: bfloat16 [6, 96, 192, 768], P(None, 'lat', None, 'chan'), may hold values from -60 to 60, as said below
- kept_lat: int32 [4], replicated, may hold values from 0 to 5, as said below
- kept_lon: int32 [4], replicated, may hold values from 0 to 5, as said below
- spec_w1: bfloat16 [2, 8, 96, 96], P(None, 'chan'), may hold values from -0.4375 to 0.4375
- spec_w2: bfloat16 [2, 8, 96, 96], P(None, 'chan'), may hold values from -0.4375 to 0.4375
- mlp_w1: bfloat16 [768, 3072], replicated, may hold values from -0.21875 to 0.21875
- mlp_w2: bfloat16 [3072, 768], replicated, may hold values from -0.109375 to 0.109375
Outputs:
- block_out: bfloat16 [6, 96, 192, 768], P(None, 'lat', None, 'chan')
Inputs may be any that keep to these rules, and one draw needn't show every extreme that they name: `fields`: finite values. `kept_lat`: 4 distinct block numbers in rising order, always holding 0 and 5. `kept_lon`: 4 distinct block numbers in rising order, always holding 0 and 5.
All inputs are finite; a program needn't handle non-finite values.
Results may differ from a plain program's by a relative error of at most 0.0065.
Values may be sent and summed in bfloat16 or wider, within the bound.
A program may use at most 128 MiB of HBM per device.

v0:
```python
import math

import jax
import jax.numpy as jnp
import numpy as np
from jax import lax
from jax.experimental import pallas as pl
from jax.experimental.pallas import tpu as pltpu
from jax.sharding import PartitionSpec as P

S, H, W, C, HID, BS = 6, 96, 192, 768, 3072, 96
L, NC = 32, 8
RH = H // L
NCH = 2
SC = S // NCH
NR = SC * RH
WS = W // NC
BOUNDS = (0, 8, 14, 18)
NT = len(BOUNDS) - 1
CUTS = {
    8: (0, 48, 96, 144, 192),
    6: (0, 40, 80, 112, 144),
    4: (0, 32, 56, 80, 96),
}
ROWS = [BOUNDS[j + 1] - BOUNDS[j] for j in range(NT)]
PACKED = [CUTS[n][3] for n in ROWS]
MAXC, MAXP = max(ROWS) * WS, max(PACKED)
TH = 64
TR = W // TH
EPS = 1e-5
F32, BF16 = jnp.float32, jnp.bfloat16
MESH = pl.DeviceIdType.MESH


def tables():
    k = np.arange(96)
    w = np.arange(W)
    angle = 2.0 * np.pi / W * ((k[:, None] * w[None, :]) % W)
    fwd = np.stack([np.cos(angle), -np.sin(angle)]) / math.sqrt(W)
    gain = np.where(k > 0, 2.0, 1.0)[:, None] / math.sqrt(W)
    inv = np.zeros((2, 96, 256))
    inv[:, :, :W] = np.stack([np.cos(angle) * gain, -np.sin(angle) * gain])
    h = (np.arange(L)[None, :] * RH + np.arange(RH)[:, None]).reshape(-1)
    angle = 2.0 * np.pi / H * ((k[:, None] * h[None, :]) % H)
    lat = np.zeros((2, 96, 128))
    lat[:, :, :H] = np.stack([np.cos(angle), np.sin(angle)]) / math.sqrt(H)
    cast = lambda t: jnp.asarray(t.reshape(2, 6, 16, -1).astype(np.float32), dtype=BF16)
    return cast(fwd), cast(inv), cast(lat)


def lanes(rows):
    return lax.broadcasted_iota(jnp.int32, (rows, 128), 1)


def fold(a0, a1, a2, a3):
    low = lanes(a0.shape[0]) < BS
    return (
        jnp.where(low, a0, pltpu.roll(a3, 96, 1)),
        jnp.where(low, a1, pltpu.roll(a3, 64, 1)),
        jnp.where(low, a2, pltpu.roll(a3, 32, 1)),
    )


def fourth(t0, t1, t2):
    lane = lanes(t0.shape[0])
    return jnp.where(
        lane < 32,
        pltpu.roll(t0, 32, 1),
        jnp.where(lane < 64, pltpu.roll(t1, 64, 1), pltpu.roll(t2, 96, 1)),
    )


def dot(a, b):
    return jnp.dot(a, b, preferred_element_type=F32)


def fold_cells(m, cuts):
    last = m[cuts[3] : cuts[4]]
    out = []
    for g in range(3):
        here = m[cuts[g] : cuts[g + 1]]
        extra = here.shape[0] - last.shape[0]
        add = jnp.concatenate([last, jnp.zeros((extra, 128), F32)], axis=0) if extra else last
        out.append(jnp.where(lanes(here.shape[0]) < BS, here, pltpu.roll(add, 96 - 32 * g, 1)))
    return jnp.concatenate(out, axis=0).astype(BF16)


def unfold_cells(t, cuts):
    t = t.astype(F32)
    parts = [t[cuts[g] : cuts[g + 1]] for g in range(3)]
    n = cuts[4] - cuts[3]
    return jnp.concatenate(parts + [fourth(*(p[0:n] for p in parts))], axis=0)


def gelu(u):
    return 0.5 * u * (1.0 + lax.erf(u * (1.0 / math.sqrt(2.0))))


def kernel(
    lat_hbm,
    lon_hbm,
    x_hbm,
    sw1_hbm,
    sw2_hbm,
    ftab_hbm,
    gtab_hbm,
    ltab_hbm,
    w1_hbm,
    w2_hbm,
    out_hbm,
    kept_lat,
    kept_lon,
    x_ref,
    sw1,
    sw2,
    ftab,
    gtab,
    ltab,
    fmat,
    gmat,
    cs,
    ct,
    sf1,
    sf2,
    w1v,
    w2v,
    st_part,
    st_in,
    nrm,
    a_scr,
    f_send,
    f_recv,
    r_scr,
    b_scr,
    sp,
    b_send,
    b_recv,
    m_scr,
    c_send,
    c_recv,
    y_scr,
    n2,
    hid,
    d_send,
    d_recv,
    o_scr,
    o_buf,
    wsem,
    isem,
    osem,
    ssem,
    rsem,
):
    lat = lax.axis_index("lat")
    chan = lax.axis_index("chan")

    half = S * RH * W // NCH
    x_loads = [
        pltpu.make_async_copy(
            x_hbm.at[pl.ds(k * half, half)], x_ref.at[pl.ds(k * half, half)], isem.at[k]
        )
        for k in range(NCH)
    ]
    small = (
        (lat_hbm, kept_lat),
        (lon_hbm, kept_lon),
        (ftab_hbm, ftab),
        (gtab_hbm, gtab),
        (ltab_hbm, ltab),
        (sw1_hbm, sw1),
        (sw2_hbm, sw2),
    )
    s_loads = [
        pltpu.make_async_copy(src, dst, isem.at[NCH + i]) for i, (src, dst) in enumerate(small)
    ]
    loads = [
        pltpu.make_async_copy(w1_hbm, w1v, wsem.at[0]),
        pltpu.make_async_copy(w2_hbm, w2v, wsem.at[1]),
    ]
    for c in x_loads:
        c.start()

    barrier = pltpu.get_barrier_semaphore()

    def greet_lat(i, carry):
        pl.semaphore_signal(
            barrier, inc=1, device_id=(lax.rem(lat + i, L), chan), device_id_type=MESH
        )
        return carry

    def greet_chan(i, carry):
        pl.semaphore_signal(
            barrier, inc=1, device_id=(lat, lax.rem(chan + i, NC)), device_id_type=MESH
        )
        return carry

    lax.fori_loop(1, L, greet_lat, 0)
    lax.fori_loop(1, NC, greet_chan, 0)
    for c in s_loads + loads:
        c.start()

    def spread_lat(src, dst, phase, k):
        pltpu.make_async_copy(src.at[k, lat], dst.at[k, lat], rsem.at[phase, k]).start()

        def go(i, carry):
            to = lax.rem(lat + i, L)
            pltpu.make_async_remote_copy(
                src_ref=src.at[k, to],
                dst_ref=dst.at[k, lat],
                send_sem=ssem.at[phase, k],
                recv_sem=rsem.at[phase, k],
                device_id=(to, chan),
                device_id_type=MESH,
            ).start()
            return carry

        lax.fori_loop(1, L, go, 0)

    def spread_chan(src, dst, phase, k, rows, same):
        part = pl.ds(0, rows)
        own = src.at[k, 0 if same else chan, part]
        pltpu.make_async_copy(own, dst.at[k, chan, part], rsem.at[phase, k]).start()

        def go(i, carry):
            to = lax.rem(chan + i, NC)
            pltpu.make_async_remote_copy(
                src_ref=src.at[k, 0 if same else to, part],
                dst_ref=dst.at[k, chan, part],
                send_sem=ssem.at[phase, k],
                recv_sem=rsem.at[phase, k],
                device_id=(lat, to),
                device_id_type=MESH,
            ).start()
            return carry

        lax.fori_loop(1, NC, go, 0)

    def arrived(dst, phase, k, count, rows):
        part = dst.at[k, pl.ds(0, count), pl.ds(0, rows)]
        pltpu.make_async_copy(part, part, rsem.at[phase, k]).wait()

    def sent(dst, phase, k, count, rows):
        part = dst.at[k, pl.ds(0, count), pl.ds(0, rows)]
        pltpu.make_async_copy(part, part, ssem.at[phase, k]).wait()

    lane = lax.broadcasted_iota(jnp.int32, (BS, 128), 1)
    left = jnp.where(lane < TH, 1.0, 0.0).astype(BF16)
    right = jnp.where(lane >= TH, 1.0, 0.0).astype(BF16)
    own_lane = lax.rem(lanes(TH), TH) == lax.broadcasted_iota(jnp.int32, (TH, 128), 0)
    st_part[...] = jnp.zeros_like(st_part)
    for k in range(NCH):
        x_loads[k].wait()
        for r in range(NR):
            xr = x_ref[pl.ds((k * NR + r) * W, W), :]
            xf = xr.astype(F32)
            sq = xf * xf
            hi = sq.astype(BF16)
            lo = (sq - hi.astype(F32)).astype(BF16)
            sums = dot(xr, left) + dot(hi, right) + dot(lo, right)
            for j in range(TR):
                row = jnp.where(own_lane, sums[j * TH : (j + 1) * TH], 0.0)
                st_part[k, 0, pl.ds(r * TR + j, 1), :] = jnp.sum(row, axis=0, keepdims=True)
        if k == 0:
            pl.semaphore_wait(barrier, L - 1 + NC - 1)
        spread_chan(st_part, st_in, 0, k, 32, True)

    for c in s_loads:
        c.wait()
    nrm[...] = jnp.zeros_like(nrm)
    a_scr[pl.ds(NR * 96, 1024 - NR * 96), :] = jnp.zeros((1024 - NR * 96, 128), F32)
    for q in range(4):
        for b in range(2):
            blk = kept_lon[(q // 2) * 2 + b]
            fmat[pl.ds(q * 32 + b * 16, 16), :] = ftab[q % 2, blk]
    g = jnp.concatenate(
        [gtab[q % 2, kept_lon[(q // 2) * 2 + b]].astype(F32) for q in range(4) for b in range(2)],
        axis=0,
    )
    gmat[...] = g.T[0:W].astype(BF16)
    t = jnp.concatenate([ltab[q, kept_lat[b]].astype(F32) for q in range(2) for b in range(4)], axis=0)
    cs[...] = t.astype(BF16)
    ct[...] = t.T[0:H].astype(BF16)
    for src, dst in ((sw1, sf1), (sw2, sf2)):
        dst[...] = jnp.zeros_like(dst)
        real, imag = src[0], src[1]
        dst[pl.ds(0, BS), pl.ds(0, BS)] = real
        dst[pl.ds(0, BS), pl.ds(128, BS)] = imag
        dst[pl.ds(128, BS), pl.ds(0, BS)] = -imag
        dst[pl.ds(128, BS), pl.ds(128, BS)] = real

    def regroup(k, dst):
        for d in range(L):
            dst[k, d] = a_scr[pl.ds(d, 32, stride=32), :].astype(BF16)

    for k in range(NCH):
        arrived(st_in, 0, k, NC, 32)
        tot = st_in[k, 0]
        for i in range(1, NC):
            tot = tot + st_in[k, i]
        tot = tot * (1.0 / C)
        var = pltpu.roll(tot, TH, 1) - tot * tot
        scale = pltpu.roll(lax.rsqrt(var + EPS), TH, 1)
        stat = jnp.where(lanes(32) < TH, tot, scale).T
        for i in range(NR * TR):
            part = pl.ds(k * NR * W + i * TH, TH)
            xf = x_ref[part, :].astype(F32)
            normed = (xf - stat[0:TH, i : i + 1]) * stat[TH : 2 * TH, i : i + 1]
            nrm[part, pl.ds(0, BS)] = normed.astype(BF16)
        side = [nrm[pl.ds((k * NR + r) * W, W), :] for r in range(NR)]
        al = dot(fmat[...], jnp.concatenate(side, axis=1))
        for r in range(NR):
            parts = fold(*(al[q * 32 : (q + 1) * 32, r * 128 : (r + 1) * 128] for q in range(4)))
            for p in range(3):
                a_scr[pl.ds((r * 3 + p) * 32, 32), :] = parts[p]
        regroup(k, f_send)
        spread_lat(f_send, f_recv, 1, k)

    for k in range(NCH):
        arrived(f_recv, 1, k, L, 32)
        for s in range(L):
            r_scr[pl.ds(s * 32, 32), :] = f_recv[k, s].astype(F32)
        for n in range(SC):
            for hh in range(RH):
                for p in range(3):
                    row = (n * RH + hh) * 3 + p
                    b_scr[pl.ds(hh * 32, 32), pl.ds((n * 3 + p) * 128, 128)] = r_scr[
                        pl.ds(row, 32, stride=32), :
                    ].astype(BF16)
        both = dot(cs[:, 0:H], b_scr[...])
        for n in range(SC):
            cols = [slice((n * 3 + p) * 128, (n * 3 + p + 1) * 128) for p in range(3)]
            co = [both[0:64, c] for c in cols]
            si = [both[64:128, c] for c in cols]
            co.append(fourth(*co))
            si.append(fourth(*si))
            for m in range(2):
                rows = pl.ds((n * 2 + m) * 64, 64)
                sp[rows, pl.ds(0, 128)] = (co[2 * m] + si[2 * m + 1]).astype(BF16)
                sp[rows, pl.ds(128, 128)] = (co[2 * m + 1] - si[2 * m]).astype(BF16)
        one = jnp.maximum(dot(sp[...], sf1[...]), 0.0).astype(BF16)
        two = dot(one, sf2[...]).astype(BF16)
        side = []
        for i in range(SC * 2):
            f = two[i * 64 : (i + 1) * 64]
            turned = jnp.concatenate([-f[:, 128:256], f[:, 0:128]], axis=1)
            side.append(jnp.concatenate([f, turned], axis=0))
        wave = dot(ct[...], jnp.concatenate(side, axis=1))
        for n in range(SC):
            parts = fold(*(wave[:, (n * 4 + q) * 128 : (n * 4 + q + 1) * 128] for q in range(4)))
            for hh in range(RH):
                for p in range(3):
                    a_scr[pl.ds(((n * RH + hh) * 3 + p) * 32, 32), :] = parts[p][
                        hh * 32 : (hh + 1) * 32
                    ]
        regroup(k, b_send)
        spread_lat(b_send, b_recv, 2, k)

    for k in range(NCH):
        arrived(b_recv, 2, k, L, 32)
        for s in range(L):
            r_scr[pl.ds(s * 32, 32), :] = b_recv[k, s].astype(F32)
        side = []
        for r in range(NR):
            parts = [r_scr[pl.ds(r * 3 + p, 32, stride=32), :] for p in range(3)]
            side.append(jnp.concatenate(parts + [fourth(*parts)], axis=0).astype(BF16))
        spectral = dot(gmat[...], jnp.concatenate(side, axis=1))
        for r in range(NR):
            at = pl.ds((k * NR + r) * W, W)
            mixed = x_ref[at, :].astype(F32) + nrm[at, pl.ds(0, BS)].astype(F32)
            mixed = mixed + spectral[:, r * 128 : r * 128 + BS]
            g = k * NR + r
            j = sum(g >= v for v in BOUNDS[1:])
            for d in range(NC):
                m_scr[d, pl.ds(g * WS, WS), pl.ds(0, BS)] = mixed[d * WS : (d + 1) * WS]
            if g == BOUNDS[j + 1] - 1:
                for d in range(NC):
                    c_send[j, d, pl.ds(0, PACKED[j]), :] = fold_cells(
                        m_scr[d, pl.ds(BOUNDS[j] * WS, ROWS[j] * WS), :], CUTS[ROWS[j]]
                    )
                spread_chan(c_send, c_recv, 3, j, PACKED[j], False)

    for c in loads:
        c.wait()
    for k in range(NT):
        arrived(c_recv, 3, k, NC, PACKED[k])
        cuts = CUTS[ROWS[k]]
        cells = ROWS[k] * WS
        lane = lanes(cells)
        acc = jnp.zeros((cells, 128), F32)
        acc2 = jnp.zeros((cells, 128), F32)
        for s in range(NC):
            y = unfold_cells(c_recv[k, s, pl.ds(0, PACKED[k]), :], cuts)
            y = jnp.where(lane < BS, y, 0.0)
            y_scr[s, pl.ds(0, cells), :] = y
            acc = acc + y
            acc2 = acc2 + y * y
        mean = jnp.sum(acc, axis=1, keepdims=True) * (1.0 / C)
        var = jnp.sum(acc2, axis=1, keepdims=True) * (1.0 / C) - mean * mean
        scale = lax.rsqrt(var + EPS)
        for i in range(2):
            z = [(y_scr[4 * i + j, pl.ds(0, cells), :] - mean) * scale for j in range(4)]
            z = [z[0]] + [pltpu.roll(z[j], 128 - 32 * j, 1) for j in range(1, 4)]
            for j in range(3):
                tile = jnp.where(lane < BS - 32 * j, z[j], z[j + 1])
                n2[pl.ds(0, cells), pl.ds((3 * i + j) * 128, 128)] = tile.astype(BF16)
        n2k = n2[pl.ds(0, cells), :]
        for i in range(HID // 512):
            cols = pl.ds(i * 512, 512)
            hid[pl.ds(0, cells), cols] = gelu(dot(n2k, w1v[:, cols])).astype(BF16)
        o = dot(hid[pl.ds(0, cells), :], w2v[...])
        tiles = [o[:, i * 128 : (i + 1) * 128] for i in range(6)]
        for s in range(NC):
            i, off = divmod(s * BS, 128)
            piece = tiles[i]
            if off:
                piece = pltpu.roll(piece, 128 - off, 1)
                if off > 32:
                    after = pltpu.roll(tiles[i + 1], 128 - off, 1)
                    piece = jnp.where(lane < 128 - off, piece, after)
            d_send[k, s, pl.ds(0, PACKED[k]), :] = fold_cells(
                y_scr[s, pl.ds(0, cells), :] + piece, cuts
            )
        spread_chan(d_send, d_recv, 4, k, PACKED[k], False)

    stores = []
    for k in range(NT):
        arrived(d_recv, 4, k, NC, PACKED[k])
        for s in range(NC):
            y = unfold_cells(d_recv[k, s, pl.ds(0, PACKED[k]), :], CUTS[ROWS[k]])
            for r in range(ROWS[k]):
                o_scr[pl.ds(r * W + s * WS, WS), :] = y[r * WS : (r + 1) * WS]
        at = pl.ds(BOUNDS[k] * W, ROWS[k] * W)
        o_buf[at, :] = o_scr[pl.ds(0, ROWS[k] * W), 0:BS].astype(BF16)
        stores.append(pltpu.make_async_copy(o_buf.at[at], out_hbm.at[at], osem.at[k]))
        stores[k].start()
    for c in stores:
        c.wait()
    for k in range(NCH):
        sent(st_in, 0, k, NC - 1, 32)
        sent(f_send, 1, k, L - 1, 32)
        sent(b_send, 2, k, L - 1, 32)
    for k in range(NT):
        sent(c_send, 3, k, NC - 1, PACKED[k])
        sent(d_send, 4, k, NC - 1, PACKED[k])


def hand_on(i_ref, o_ref, buf, sem_in, sem_out):
    step = i_ref.shape[0] // 6
    parts = [pl.ds(i * step, step) for i in range(6)]
    reads = [pltpu.make_async_copy(i_ref.at[p], buf.at[p], sem_in.at[i]) for i, p in enumerate(parts)]
    writes = [pltpu.make_async_copy(buf.at[p], o_ref.at[p], sem_out.at[i]) for i, p in enumerate(parts)]
    for c in reads:
        c.start()
    for r, w in zip(reads, writes):
        r.wait()
        w.start()
    for c in writes:
        c.wait()


def on_device(fields, kept_lat, kept_lon, spec_w1, spec_w2, mlp_w1, mlp_w2):
    fwd, inv, lat = tables()
    hbm = pl.BlockSpec(memory_space=pltpu.HBM)
    cells = S * RH * W
    parts = pl.pallas_call(
        kernel,
        out_shape=jax.ShapeDtypeStruct((cells, BS), BF16),
        in_specs=[hbm] * 10,
        out_specs=hbm,
        scratch_shapes=[
            pltpu.SMEM((4,), jnp.int32),
            pltpu.SMEM((4,), jnp.int32),
            pltpu.VMEM((cells, BS), BF16),
            pltpu.VMEM((2, BS, BS), BF16),
            pltpu.VMEM((2, BS, BS), BF16),
            pltpu.VMEM(fwd.shape, BF16),
            pltpu.VMEM(inv.shape, BF16),
            pltpu.VMEM(lat.shape, BF16),
            pltpu.VMEM((128, W), BF16),
            pltpu.VMEM((W, 128), BF16),
            pltpu.VMEM((128, 128), BF16),
            pltpu.VMEM((H, 128), BF16),
            pltpu.VMEM((256, 256), BF16),
            pltpu.VMEM((256, 256), BF16),
            pltpu.VMEM((C, HID), BF16),
            pltpu.VMEM((HID, C), BF16),
            pltpu.VMEM((NCH, 1, 32, 128), F32),
            pltpu.VMEM((NCH, NC, 32, 128), F32),
            pltpu.VMEM((cells, 128), BF16),
            pltpu.VMEM((1024, 128), F32),
            pltpu.VMEM((NCH, L, 32, 128), BF16),
            pltpu.VMEM((NCH, L, 32, 128), BF16),
            pltpu.VMEM((1024, 128), F32),
            pltpu.VMEM((H, SC * 384), BF16),
            pltpu.VMEM((SC * 128, 256), BF16),
            pltpu.VMEM((NCH, L, 32, 128), BF16),
            pltpu.VMEM((NCH, L, 32, 128), BF16),
            pltpu.VMEM((NC, S * RH * WS, 128), F32),
            pltpu.VMEM((NT, NC, MAXP, 128), BF16),
            pltpu.VMEM((NT, NC, MAXP, 128), BF16),
            pltpu.VMEM((NC, MAXC, 128), F32),
            pltpu.VMEM((MAXC, C), BF16),
            pltpu.VMEM((MAXC, HID), BF16),
            pltpu.VMEM((NT, NC, MAXP, 128), BF16),
            pltpu.VMEM((NT, NC, MAXP, 128), BF16),
            pltpu.VMEM((max(ROWS) * W, 128), F32),
            pltpu.VMEM((cells, BS), BF16),
            pltpu.SemaphoreType.DMA((2,)),
            pltpu.SemaphoreType.DMA((NCH + 7,)),
            pltpu.SemaphoreType.DMA((NT,)),
            pltpu.SemaphoreType.DMA((5, NT)),
            pltpu.SemaphoreType.DMA((5, NT)),
        ],
        compiler_params=pltpu.CompilerParams(
            collective_id=0, has_side_effects=True, vmem_limit_bytes=56 * 1024 * 1024
        ),
        cost_estimate=pl.CostEstimate(
            flops=5_000_000_000, bytes_accessed=12_000_000, transcendentals=1_400_000
        ),
    )(
        kept_lat,
        kept_lon,
        fields.reshape(cells, BS),
        spec_w1.reshape(2, BS, BS),
        spec_w2.reshape(2, BS, BS),
        fwd,
        inv,
        lat,
        mlp_w1,
        mlp_w2,
    )
    out = pl.pallas_call(
        hand_on,
        out_shape=jax.ShapeDtypeStruct((cells, BS), BF16),
        in_specs=[pl.BlockSpec(memory_space=pltpu.HBM)],
        out_specs=pl.BlockSpec(memory_space=pltpu.HBM),
        scratch_shapes=[
            pltpu.VMEM((cells, BS), BF16),
            pltpu.SemaphoreType.DMA((6,)),
            pltpu.SemaphoreType.DMA((6,)),
        ],
    )(parts)
    return out.reshape(S, RH, W, BS)


def solution(mesh):
    placed = (
        P(None, "lat", None, "chan"),
        P(),
        P(),
        P(None, "chan", None, None),
        P(None, "chan", None, None),
        P(),
        P(),
    )
    return jax.shard_map(
        on_device,
        mesh=mesh,
        in_specs=placed,
        out_specs=P(None, "lat", None, "chan"),
        check_vma=False,
    )
```

profile of v0, /device:TPU:1, one launch (start us, length us, event | category | flops | bytes accessed | tf_op | source)
XLA Modules:
  0.0 61.3 jit_solution(8251490809444336882)
XLA Ops:
  0.0 59.3 %shard_map.100.i_ref = bf16[3456,96]{1,0:T(8,128)(2,1)} custom-call(s32[4]{0:T(128)} %lat_hbm.1, s32[4]{0:T(128)} %lon_hbm.1, bf16[3456,96]{1,0:T(8,128)(2,1)} %bitcast.4, bf16[2,96,96]{2,1,0:T(8,128)(2,1)} %bitcast.5, bf16[2,96,96]{2,1,0:T(8,128)(2,1)} %bitcast.6, bf16[2,6,16,192]{3,2,1,0:T(8,128)(2,1)} %constant.6.clone.ftab_hbm, ...), custom_call_target="tpu_custom_call" | custom-call | flops 5000000000 | bytes 12000000 | tf_op jit(solution)/shard_map/pallas_call | solution.py:465
  59.3 2.0 %shard_map.101 = bf16[3456,96]{1,0:T(8,128)(2,1)} custom-call(bf16[3456,96]{1,0:T(8,128)(2,1)} %shard_map.100.i_ref), custom_call_target="tpu_custom_call" | custom-call | tf_op jit(solution)/shard_map/pallas_call | solution.py:532
where the time goes:
time: 62.4 us; the launch traced here: 61.3 us
  Pallas kernels  61.3 us (98%)
    pallas_call x1, Pallas kernels, on_device(): pl.pallas_call(kernel, out_shape=jax.ShapeDtypeStruct((cells, BS), BF16),...  59.3 us
    pallas_call x1, Pallas kernels, on_device(): pl.pallas_call(hand_on, out_shape=jax.ShapeDtypeStruct((cells, BS), BF16)...  2.02 us

commit v1 on v0

--- a/solution.py
+++ b/solution.py
@@ -13,7 +13,10 @@
 RH = H // L
 NCH = 2
 SC = S // NCH
-NR = SC * RH
+NG = S * RH
+NB = 7
+OUT_PAIRS, OUT_BLOCKS = (0, 11, 18), (0, 4, 7)
+BACK_PAIRS, BACK_BLOCKS = (0, 8, 18), (0, 3, 7)
 WS = W // NC
 BOUNDS = (0, 8, 14, 18)
 NT = len(BOUNDS) - 1
@@ -27,6 +30,7 @@
 MAXC, MAXP = max(ROWS) * WS, max(PACKED)
 TH = 64
 TR = W // TH
+STAT_ROWS = (40, 24)
 EPS = 1e-5
 F32, BF16 = jnp.float32, jnp.bfloat16
 MESH = pl.DeviceIdType.MESH
@@ -154,12 +158,12 @@
     lat = lax.axis_index("lat")
     chan = lax.axis_index("chan")
 
-    half = S * RH * W // NCH
+    x_parts = [
+        pl.ds(OUT_PAIRS[k] * W, (OUT_PAIRS[k + 1] - OUT_PAIRS[k]) * W) for k in range(NCH)
+    ]
     x_loads = [
-        pltpu.make_async_copy(
-            x_hbm.at[pl.ds(k * half, half)], x_ref.at[pl.ds(k * half, half)], isem.at[k]
-        )
-        for k in range(NCH)
+        pltpu.make_async_copy(x_hbm.at[part], x_ref.at[part], isem.at[k])
+        for k, part in enumerate(x_parts)
     ]
     small = (
         (lat_hbm, kept_lat),
@@ -199,14 +203,15 @@
     for c in s_loads + loads:
         c.start()
 
-    def spread_lat(src, dst, phase, k):
-        pltpu.make_async_copy(src.at[k, lat], dst.at[k, lat], rsem.at[phase, k]).start()
+    def spread_lat(src, dst, phase, k, bounds):
+        part = pl.ds(bounds[k], bounds[k + 1] - bounds[k])
+        pltpu.make_async_copy(src.at[lat, part], dst.at[lat, part], rsem.at[phase, k]).start()
 
         def go(i, carry):
             to = lax.rem(lat + i, L)
             pltpu.make_async_remote_copy(
-                src_ref=src.at[k, to],
-                dst_ref=dst.at[k, lat],
+                src_ref=src.at[to, part],
+                dst_ref=dst.at[lat, part],
                 send_sem=ssem.at[phase, k],
                 recv_sem=rsem.at[phase, k],
                 device_id=(to, chan),
@@ -215,6 +220,22 @@
             return carry
 
         lax.fori_loop(1, L, go, 0)
+
+    def arrived_lat(dst, phase, k, bounds):
+        part = dst.at[pl.ds(0, L), pl.ds(bounds[k], bounds[k + 1] - bounds[k])]
+        pltpu.make_async_copy(part, part, rsem.at[phase, k]).wait()
+        for s in range(L):
+            for b in range(bounds[k], bounds[k + 1]):
+                r_scr[pl.ds((s * NB + b) * 8, 8), :] = dst[s, b].astype(F32)
+
+    def sent_lat(dst, phase, k, bounds):
+        part = dst.at[pl.ds(0, L - 1), pl.ds(bounds[k], bounds[k + 1] - bounds[k])]
+        pltpu.make_async_copy(part, part, ssem.at[phase, k]).wait()
+
+    def regroup(dst, k, bounds):
+        for d in range(L):
+            for b in range(bounds[k], bounds[k + 1]):
+                dst[d, b] = a_scr[pl.ds(b * 256 + d, 8, stride=32), :].astype(BF16)
 
     def spread_chan(src, dst, phase, k, rows, same):
         part = pl.ds(0, rows)
@@ -250,8 +271,8 @@
     st_part[...] = jnp.zeros_like(st_part)
     for k in range(NCH):
         x_loads[k].wait()
-        for r in range(NR):
-            xr = x_ref[pl.ds((k * NR + r) * W, W), :]
+        for g in range(OUT_PAIRS[k], OUT_PAIRS[k + 1]):
+            xr = x_ref[pl.ds(g * W, W), :]
             xf = xr.astype(F32)
             sq = xf * xf
             hi = sq.astype(BF16)
@@ -259,15 +280,15 @@
             sums = dot(xr, left) + dot(hi, right) + dot(lo, right)
             for j in range(TR):
                 row = jnp.where(own_lane, sums[j * TH : (j + 1) * TH], 0.0)
-                st_part[k, 0, pl.ds(r * TR + j, 1), :] = jnp.sum(row, axis=0, keepdims=True)
+                st_part[k, 0, pl.ds((g - OUT_PAIRS[k]) * TR + j, 1), :] = jnp.sum(row, axis=0, keepdims=True)
         if k == 0:
             pl.semaphore_wait(barrier, L - 1 + NC - 1)
-        spread_chan(st_part, st_in, 0, k, 32, True)
+        spread_chan(st_part, st_in, 0, k, STAT_ROWS[k], True)
 
     for c in s_loads:
         c.wait()
     nrm[...] = jnp.zeros_like(nrm)
-    a_scr[pl.ds(NR * 96, 1024 - NR * 96), :] = jnp.zeros((1024 - NR * 96, 128), F32)
+    a_scr[pl.ds(NG * 96, 64), :] = jnp.zeros((64, 128), F32)
     for q in range(4):
         for b in range(2):
             blk = kept_lon[(q // 2) * 2 + b]
@@ -288,43 +309,39 @@
         dst[pl.ds(128, BS), pl.ds(0, BS)] = -imag
         dst[pl.ds(128, BS), pl.ds(128, BS)] = real
 
-    def regroup(k, dst):
-        for d in range(L):
-            dst[k, d] = a_scr[pl.ds(d, 32, stride=32), :].astype(BF16)
-
     for k in range(NCH):
-        arrived(st_in, 0, k, NC, 32)
-        tot = st_in[k, 0]
+        arrived(st_in, 0, k, NC, STAT_ROWS[k])
+        rows = pl.ds(0, STAT_ROWS[k])
+        tot = st_in[k, 0, rows, :]
         for i in range(1, NC):
-            tot = tot + st_in[k, i]
+            tot = tot + st_in[k, i, rows, :]
         tot = tot * (1.0 / C)
         var = pltpu.roll(tot, TH, 1) - tot * tot
         scale = pltpu.roll(lax.rsqrt(var + EPS), TH, 1)
-        stat = jnp.where(lanes(32) < TH, tot, scale).T
-        for i in range(NR * TR):
-            part = pl.ds(k * NR * W + i * TH, TH)
+        stat = jnp.where(lanes(STAT_ROWS[k]) < TH, tot, scale).T
+        pairs = range(OUT_PAIRS[k], OUT_PAIRS[k + 1])
+        for i in range(len(pairs) * TR):
+            part = pl.ds(pairs[0] * W + i * TH, TH)
             xf = x_ref[part, :].astype(F32)
             normed = (xf - stat[0:TH, i : i + 1]) * stat[TH : 2 * TH, i : i + 1]
             nrm[part, pl.ds(0, BS)] = normed.astype(BF16)
-        side = [nrm[pl.ds((k * NR + r) * W, W), :] for r in range(NR)]
+        side = [nrm[pl.ds(g * W, W), :] for g in pairs]
         al = dot(fmat[...], jnp.concatenate(side, axis=1))
-        for r in range(NR):
+        for r, g in enumerate(pairs):
             parts = fold(*(al[q * 32 : (q + 1) * 32, r * 128 : (r + 1) * 128] for q in range(4)))
             for p in range(3):
-                a_scr[pl.ds((r * 3 + p) * 32, 32), :] = parts[p]
-        regroup(k, f_send)
-        spread_lat(f_send, f_recv, 1, k)
+                a_scr[pl.ds((g * 3 + p) * 32, 32), :] = parts[p]
+        regroup(f_send, k, OUT_BLOCKS)
+        spread_lat(f_send, f_recv, 1, k, OUT_BLOCKS)
 
     for k in range(NCH):
-        arrived(f_recv, 1, k, L, 32)
-        for s in range(L):
-            r_scr[pl.ds(s * 32, 32), :] = f_recv[k, s].astype(F32)
+        arrived_lat(f_recv, 1, k, OUT_BLOCKS)
         for n in range(SC):
             for hh in range(RH):
                 for p in range(3):
-                    row = (n * RH + hh) * 3 + p
+                    row = ((k * SC + n) * RH + hh) * 3 + p
                     b_scr[pl.ds(hh * 32, 32), pl.ds((n * 3 + p) * 128, 128)] = r_scr[
-                        pl.ds(row, 32, stride=32), :
+                        pl.ds(row, 32, stride=NB * 8), :
                     ].astype(BF16)
         both = dot(cs[:, 0:H], b_scr[...])
         for n in range(SC):
@@ -349,26 +366,23 @@
             parts = fold(*(wave[:, (n * 4 + q) * 128 : (n * 4 + q + 1) * 128] for q in range(4)))
             for hh in range(RH):
                 for p in range(3):
-                    a_scr[pl.ds(((n * RH + hh) * 3 + p) * 32, 32), :] = parts[p][
-                        hh * 32 : (hh + 1) * 32
-                    ]
-        regroup(k, b_send)
-        spread_lat(b_send, b_recv, 2, k)
+                    row = ((k * SC + n) * RH + hh) * 3 + p
+                    a_scr[pl.ds(row * 32, 32), :] = parts[p][hh * 32 : (hh + 1) * 32]
+        regroup(b_send, k, BACK_BLOCKS)
+        spread_lat(b_send, b_recv, 2, k, BACK_BLOCKS)
 
     for k in range(NCH):
-        arrived(b_recv, 2, k, L, 32)
-        for s in range(L):
-            r_scr[pl.ds(s * 32, 32), :] = b_recv[k, s].astype(F32)
+        arrived_lat(b_recv, 2, k, BACK_BLOCKS)
+        pairs = range(BACK_PAIRS[k], BACK_PAIRS[k + 1])
         side = []
-        for r in range(NR):
-            parts = [r_scr[pl.ds(r * 3 + p, 32, stride=32), :] for p in range(3)]
+        for g in pairs:
+            parts = [r_scr[pl.ds(g * 3 + p, 32, stride=NB * 8), :] for p in range(3)]
             side.append(jnp.concatenate(parts + [fourth(*parts)], axis=0).astype(BF16))
         spectral = dot(gmat[...], jnp.concatenate(side, axis=1))
-        for r in range(NR):
-            at = pl.ds((k * NR + r) * W, W)
+        for r, g in enumerate(pairs):
+            at = pl.ds(g * W, W)
             mixed = x_ref[at, :].astype(F32) + nrm[at, pl.ds(0, BS)].astype(F32)
             mixed = mixed + spectral[:, r * 128 : r * 128 + BS]
-            g = k * NR + r
             j = sum(g >= v for v in BOUNDS[1:])
             for d in range(NC):
                 m_scr[d, pl.ds(g * WS, WS), pl.ds(0, BS)] = mixed[d * WS : (d + 1) * WS]
@@ -430,29 +444,30 @@
             for r in range(ROWS[k]):
                 o_scr[pl.ds(r * W + s * WS, WS), :] = y[r * WS : (r + 1) * WS]
         at = pl.ds(BOUNDS[k] * W, ROWS[k] * W)
-        o_buf[at, :] = o_scr[pl.ds(0, ROWS[k] * W), 0:BS].astype(BF16)
+        o_buf[at, :] = o_scr[pl.ds(0, ROWS[k] * W), :].astype(BF16)
         stores.append(pltpu.make_async_copy(o_buf.at[at], out_hbm.at[at], osem.at[k]))
         stores[k].start()
     for c in stores:
         c.wait()
     for k in range(NCH):
-        sent(st_in, 0, k, NC - 1, 32)
-        sent(f_send, 1, k, L - 1, 32)
-        sent(b_send, 2, k, L - 1, 32)
+        sent(st_in, 0, k, NC - 1, STAT_ROWS[k])
+        sent_lat(f_send, 1, k, OUT_BLOCKS)
+        sent_lat(b_send, 2, k, BACK_BLOCKS)
     for k in range(NT):
         sent(c_send, 3, k, NC - 1, PACKED[k])
         sent(d_send, 4, k, NC - 1, PACKED[k])
 
 
-def hand_on(i_ref, o_ref, buf, sem_in, sem_out):
+def hand_on(i_ref, o_ref, buf, narrow, sem_in, sem_out):
     step = i_ref.shape[0] // 6
     parts = [pl.ds(i * step, step) for i in range(6)]
     reads = [pltpu.make_async_copy(i_ref.at[p], buf.at[p], sem_in.at[i]) for i, p in enumerate(parts)]
-    writes = [pltpu.make_async_copy(buf.at[p], o_ref.at[p], sem_out.at[i]) for i, p in enumerate(parts)]
+    writes = [pltpu.make_async_copy(narrow.at[p], o_ref.at[p], sem_out.at[i]) for i, p in enumerate(parts)]
     for c in reads:
         c.start()
-    for r, w in zip(reads, writes):
+    for p, r, w in zip(parts, reads, writes):
         r.wait()
+        narrow[p, :] = buf[p, 0:BS]
         w.start()
     for c in writes:
         c.wait()
@@ -464,7 +479,7 @@
     cells = S * RH * W
     parts = pl.pallas_call(
         kernel,
-        out_shape=jax.ShapeDtypeStruct((cells, BS), BF16),
+        out_shape=jax.ShapeDtypeStruct((cells, 128), BF16),
         in_specs=[hbm] * 10,
         out_specs=hbm,
         scratch_shapes=[
@@ -484,17 +499,17 @@
             pltpu.VMEM((256, 256), BF16),
             pltpu.VMEM((C, HID), BF16),
             pltpu.VMEM((HID, C), BF16),
-            pltpu.VMEM((NCH, 1, 32, 128), F32),
-            pltpu.VMEM((NCH, NC, 32, 128), F32),
+            pltpu.VMEM((NCH, 1, STAT_ROWS[0], 128), F32),
+            pltpu.VMEM((NCH, NC, STAT_ROWS[0], 128), F32),
             pltpu.VMEM((cells, 128), BF16),
-            pltpu.VMEM((1024, 128), F32),
-            pltpu.VMEM((NCH, L, 32, 128), BF16),
-            pltpu.VMEM((NCH, L, 32, 128), BF16),
-            pltpu.VMEM((1024, 128), F32),
+            pltpu.VMEM((NB * 256, 128), F32),
+            pltpu.VMEM((L, NB, 8, 128), BF16),
+            pltpu.VMEM((L, NB, 8, 128), BF16),
+            pltpu.VMEM((NB * 256, 128), F32),
             pltpu.VMEM((H, SC * 384), BF16),
             pltpu.VMEM((SC * 128, 256), BF16),
-            pltpu.VMEM((NCH, L, 32, 128), BF16),
-            pltpu.VMEM((NCH, L, 32, 128), BF16),
+            pltpu.VMEM((L, NB, 8, 128), BF16),
+            pltpu.VMEM((L, NB, 8, 128), BF16),
             pltpu.VMEM((NC, S * RH * WS, 128), F32),
             pltpu.VMEM((NT, NC, MAXP, 128), BF16),
             pltpu.VMEM((NT, NC, MAXP, 128), BF16),
@@ -504,7 +519,7 @@
             pltpu.VMEM((NT, NC, MAXP, 128), BF16),
             pltpu.VMEM((NT, NC, MAXP, 128), BF16),
             pltpu.VMEM((max(ROWS) * W, 128), F32),
-            pltpu.VMEM((cells, BS), BF16),
+            pltpu.VMEM((cells, 128), BF16),
             pltpu.SemaphoreType.DMA((2,)),
             pltpu.SemaphoreType.DMA((NCH + 7,)),
             pltpu.SemaphoreType.DMA((NT,)),
@@ -535,6 +550,7 @@
         in_specs=[pl.BlockSpec(memory_space=pltpu.HBM)],
         out_specs=pl.BlockSpec(memory_space=pltpu.HBM),
         scratch_shapes=[
+            pltpu.VMEM((cells, 128), BF16),
             pltpu.VMEM((cells, BS), BF16),
             pltpu.SemaphoreType.DMA((6,)),
             pltpu.SemaphoreType.DMA((6,)),

time: 62.4 us -> 61.1 us (0.979); the launches traced: 61.3 us -> 61 us
  no operation moved by 1% of the time
where the time goes in v1:
time: 61.1 us; the launch traced here: 61 us
  Pallas kernels  61 us (100%)
    pallas_call x1, Pallas kernels, on_device(): pl.pallas_call(kernel, out_shape=jax.ShapeDtypeStruct((cells, 128), BF16)...  58.9 us
    pallas_call x1, Pallas kernels, on_device(): pl.pallas_call(hand_on, out_shape=jax.ShapeDtypeStruct((cells, BS), BF16)...  2.04 us

profile of v1, /device:TPU:1, one launch (start us, length us, event | category | flops | bytes accessed | tf_op | source)
XLA Modules:
  0.0 61.0 jit_solution(1584365376548852201)
XLA Ops:
  0.0 58.9 %shard_map.100.i_ref = bf16[3456,128]{1,0:T(8,128)(2,1)} custom-call(s32[4]{0:T(128)} %lat_hbm.1, s32[4]{0:T(128)} %lon_hbm.1, bf16[3456,96]{1,0:T(8,128)(2,1)} %bitcast.4, bf16[2,96,96]{2,1,0:T(8,128)(2,1)} %bitcast.5, bf16[2,96,96]{2,1,0:T(8,128)(2,1)} %bitcast.6, bf16[2,6,16,192]{3,2,1,0:T(8,128)(2,1)} %constant.6.clone.ftab_hbm, ...), custom_call_target="tpu_custom_call" | custom-call | flops 5000000000 | bytes 12000000 | tf_op jit(solution)/shard_map/pallas_call | solution.py:480
  58.9 2.0 %shard_map.101 = bf16[3456,96]{1,0:T(8,128)(2,1)} custom-call(bf16[3456,128]{1,0:T(8,128)(2,1)} %shard_map.100.i_ref), custom_call_target="tpu_custom_call" | custom-call | tf_op jit(solution)/shard_map/pallas_call | solution.py:547

commit v2 on v1

--- a/solution.py
+++ b/solution.py
@@ -18,11 +18,12 @@
 OUT_PAIRS, OUT_BLOCKS = (0, 11, 18), (0, 4, 7)
 BACK_PAIRS, BACK_BLOCKS = (0, 8, 18), (0, 3, 7)
 WS = W // NC
-BOUNDS = (0, 8, 14, 18)
+BOUNDS = (0, 8, 13, 18)
 NT = len(BOUNDS) - 1
 CUTS = {
     8: (0, 48, 96, 144, 192),
     6: (0, 40, 80, 112, 144),
+    5: (0, 32, 64, 96, 120),
     4: (0, 32, 56, 80, 96),
 }
 ROWS = [BOUNDS[j + 1] - BOUNDS[j] for j in range(NT)]

time: 61.1 us -> 61.1 us (level)
  no operation moved by 1% of the time
where the time goes in v2:
time: 61.1 us; the launch traced here: 60.9 us
  Pallas kernels  60.9 us (100%)
    pallas_call x1, Pallas kernels, on_device(): pl.pallas_call(kernel, out_shape=jax.ShapeDtypeStruct((cells, 128), BF16)...  58.9 us
    pallas_call x1, Pallas kernels, on_device(): pl.pallas_call(hand_on, out_shape=jax.ShapeDtypeStruct((cells, BS), BF16)...  2.04 us

profile of v2, /device:TPU:1, one launch (start us, length us, event | category | flops | bytes accessed | tf_op | source)
XLA Modules:
  0.0 60.9 jit_solution(4034665516435165863)
XLA Ops:
  0.0 58.9 %shard_map.100.i_ref = bf16[3456,128]{1,0:T(8,128)(2,1)} custom-call(s32[4]{0:T(128)} %lat_hbm.1, s32[4]{0:T(128)} %lon_hbm.1, bf16[3456,96]{1,0:T(8,128)(2,1)} %bitcast.4, bf16[2,96,96]{2,1,0:T(8,128)(2,1)} %bitcast.5, bf16[2,96,96]{2,1,0:T(8,128)(2,1)} %bitcast.6, bf16[2,6,16,192]{3,2,1,0:T(8,128)(2,1)} %constant.6.clone.ftab_hbm, ...), custom_call_target="tpu_custom_call" | custom-call | flops 5000000000 | bytes 12000000 | tf_op jit(solution)/shard_map/pallas_call | solution.py:481
  58.9 2.0 %shard_map.101 = bf16[3456,96]{1,0:T(8,128)(2,1)} custom-call(bf16[3456,128]{1,0:T(8,128)(2,1)} %shard_map.100.i_ref), custom_call_target="tpu_custom_call" | custom-call | tf_op jit(solution)/shard_map/pallas_call | solution.py:548
